TPU v7x, 32 devices: a whole 2x2x4 slice. The times are simulated.
32 devices in a mesh: level: 2 (over y), lon: 8 (over z, x), lat: 2 (over core).
Axes of the slice: x: 2, y: 2, z: 4, core: 2. Of those that a mesh axis runs over, the one named last changes fastest.
Arguments:
- wind_snaps: float32 [4, 32, 32, 256], P('level', None, 'lon', 'lat'), parts along dimension 0, may hold values from -48 to 48
- old_basis: float32 [4, 64, 32, 256], P('level', None, 'lon', 'lat'), parts along dimension 0, may hold values from -17 to 17
- old_values: float32 [4, 64], P('level'), parts along dimension 0, may hold values from 1 to 4
Outputs:
- new_basis: float32 [4, 64, 32, 256], P('level', None, 'lon', 'lat'), parts along dimension 0
- new_values: float32 [4, 64], P('level'), parts along dimension 0
There are 2 independent parts, one for each index of `level`. A program takes and returns all parts, laid end to end along the dimension named above; each array names one. Nothing has to cross between parts.
All inputs are finite; a program needn't handle non-finite values.
Results may differ from a plain program's by a relative error of at most 0.00012.
Values sent between devices are 32-bit elements; how exact they have to be, the bound alone decides.
A program may use at most 64 MiB of HBM per device.

v0:
```python
import jax
import jax.numpy as jnp
from jax import lax
from jax.sharding import PartitionSpec as P

ITERS = 2


FULL_PRECISION = lax.Precision.HIGHEST


def extended(value, sides, width, wrap):
    for axis, dim in sides:
        count, length = (lax.axis_size(axis), value.shape[dim])
        up = [(i, (i + 1) % count) for i in range(count if wrap else count - 1)]
        down = [(j, i) for i, j in up]
        last = lax.slice_in_dim(value, length - width, length, axis=dim)
        first = lax.slice_in_dim(value, 0, width, axis=dim)
        before = lax.ppermute(last, axis, up)
        after = lax.ppermute(first, axis, down)
        value = jnp.concatenate([before, value, after], axis=dim)
    return value


def cholesky_pair(matrix):
    order = matrix.shape[0]
    positions = jnp.arange(order, dtype=jnp.int32)

    def row_step(row, carry):
        lower, inverse = carry
        column = lax.dynamic_slice_in_dim(matrix, row, 1, 1)[:, 0]
        partial_row = jnp.dot(inverse, column, precision=FULL_PRECISION)
        diag_entry = lax.dynamic_slice_in_dim(column, row, 1, 0)[0]
        pivot = jnp.sqrt(diag_entry - jnp.sum(partial_row * partial_row))
        unit = (positions == row).astype(matrix.dtype)
        lower_row = partial_row + pivot * unit
        inverse_row = (unit - jnp.dot(partial_row, inverse, precision=FULL_PRECISION)) / pivot
        lower = lax.dynamic_update_slice_in_dim(lower, lower_row[None], row, 0)
        inverse = lax.dynamic_update_slice_in_dim(inverse, inverse_row[None], row, 0)
        return (lower, inverse)

    return lax.fori_loop(0, order, row_step, (jnp.zeros_like(matrix), jnp.zeros_like(matrix)))


def project_one(gram_uu, gram_ua):
    factor_low, low_inverse = cholesky_pair(gram_uu)
    projected = jnp.dot(low_inverse, gram_ua, precision=FULL_PRECISION)
    lifted = jnp.dot(low_inverse.T, projected, precision=FULL_PRECISION)
    return (low_inverse, projected, lifted)


def upper_pair(gram):
    lower, inverse = cholesky_pair(gram)
    return (lower.T, inverse.T)


def rotate_one(low_inverse, projected, factor_up, up_inverse, values):
    rank_count = values.shape[0]
    snap_count = factor_up.shape[0]
    top_rows = jnp.concatenate([jnp.diag(values), projected], axis=1)
    bottom_rows = jnp.concatenate(
        [jnp.zeros((snap_count, rank_count), jnp.float32), factor_up], axis=1
    )
    joint_matrix = jnp.concatenate([top_rows, bottom_rows], axis=0)
    square = jnp.dot(joint_matrix, joint_matrix.T, precision=FULL_PRECISION)
    subspace = jnp.eye(rank_count + snap_count, rank_count, dtype=jnp.float32)
    for sweep in range(ITERS):
        applied = jnp.dot(square, subspace, precision=FULL_PRECISION)
        inner = jnp.dot(applied.T, applied, precision=FULL_PRECISION)
        chol_low, chol_inverse = cholesky_pair(inner)
        subspace = jnp.dot(applied, chol_inverse.T, precision=FULL_PRECISION)
    energy = jnp.sum(subspace * jnp.dot(square, subspace, precision=FULL_PRECISION), axis=0)
    new_values = jnp.sqrt(energy)
    mix_old = jnp.dot(low_inverse.T, subspace[:rank_count], precision=FULL_PRECISION).T
    mix_new = jnp.dot(up_inverse, subspace[rank_count:], precision=FULL_PRECISION).T
    return (mix_old, mix_new, new_values)


def residual_rows(fields, basis_rows, lifted):
    return fields - jnp.einsum("fks,fkc->fsc", lifted, basis_rows, precision=FULL_PRECISION)


def per_device(wind_snaps, old_basis, old_values):
    snap_count = wind_snaps.shape[1]
    rank_count = old_basis.shape[1]
    lon_cells = wind_snaps.shape[2]
    lat_cells = wind_snaps.shape[3]
    rows_all = lat_cells * lax.axis_size("lat")
    cell_count = lon_cells * lax.axis_size("lon") * rows_all
    row_place = (lax.axis_index("lat") * lat_cells + jnp.arange(lat_cells, dtype=jnp.int32)).astype(
        jnp.float32
    )
    cosines = jnp.cos(((row_place + 0.5) / rows_all - 0.5) * (jnp.pi / 2.0))
    lon_padded = extended(wind_snaps, (("lon", 2),), 1, True)
    lat_padded = extended(wind_snaps * cosines, (("lat", 3),), 1, False)
    lon_diff = lon_padded[:, :, 2:, :] - lon_padded[:, :, :-2, :]
    lat_diff = lat_padded[:, :, :, 2:] - lat_padded[:, :, :, :-2]
    twice_cos = 2.0 * cosines
    vorticity = (lon_diff[1] - lat_diff[0]) / twice_cos
    divergence = (lon_diff[0] + lat_diff[1]) / twice_cos
    fields = jnp.stack([vorticity, divergence]).reshape(2, snap_count, lon_cells * lat_cells)
    basis_rows = old_basis.reshape(2, rank_count, lon_cells * lat_cells)
    local_uu = jnp.einsum("fkc,fjc->fkj", basis_rows, basis_rows, precision=FULL_PRECISION)
    local_ua = jnp.einsum("fkc,fsc->fks", basis_rows, fields, precision=FULL_PRECISION)
    sum_uu, sum_ua = lax.psum((local_uu, local_ua), ("lon", "lat"))
    low_inverse, projected, lifted = jax.vmap(project_one)(sum_uu / cell_count, sum_ua / cell_count)
    residual = residual_rows(fields, basis_rows, lifted)
    local_rr = jnp.einsum("fsc,ftc->fst", residual, residual, precision=FULL_PRECISION)
    sum_rr = lax.psum(local_rr, ("lon", "lat"))
    factor_up, up_inverse = jax.vmap(upper_pair)(sum_rr / cell_count)
    mix_old, mix_new, new_values = jax.vmap(rotate_one)(
        low_inverse, projected, factor_up, up_inverse, old_values
    )
    new_basis = jnp.einsum("fkj,fjc->fkc", mix_old, basis_rows, precision=FULL_PRECISION)
    new_basis = new_basis + jnp.einsum("fks,fsc->fkc", mix_new, residual, precision=FULL_PRECISION)
    return (new_basis.reshape(2, rank_count, lon_cells, lat_cells), new_values)


def solution(mesh):
    placed = (P("level", None, "lon", "lat"), P("level", None, "lon", "lat"), P("level", None))
    return jax.shard_map(
        per_device,
        mesh=mesh,
        in_specs=placed,
        out_specs=(P("level", None, "lon", "lat"), P("level", None)),
        check_vma=False,
    )
```

profile of v0, /device:TPU:0, one launch (start us, length us, event | category | flops | bytes accessed | tf_op | source)
XLA Modules:
  0.0 1083.0 jit_solution(2098849238049554596)
XLA Ops:
  0.6 1.0 fusion.76
  1.7 6.0 collective-permute-start
  7.7 1.1 reshape.448
  10.0 4.3 collective-permute-done.1
  14.3 1.2 fusion.47
  15.7 1.3 collective-permute-start.2
  17.0 3.0 collective-permute-start.3
  20.1 0.9 collective-permute-done.3
  21.7 58.7 %all-reduce.1 = (f32[2,64,64]{2,1,0:T(8,128)S(1)}, f32[2,64,32]{1,2,0:T(8,128)S(1)}) all-reduce(f32[2,64,64]{2,1,0:T(8,128)S(1)} %fusion.78, f32[2,64,32]{1,2,0:T(8,128)S(1)} %convolution_bitcast_fusion), channel_id=1, replica_groups=mesh['level'=2,'lon'=8,'lat'=2] {'lon','lat'}, use_global_device_ids=true, to_apply=%region_0.0 | all-reduce | flops 12288 | bytes 98304 | tf_op jit(solution)/shard_map/psum | solution.py:105
  81.2 268.9 %while.71 = (s32[]{:T(128)}, f32[2,64,64]{2,0,1:T(2,128)S(1)}, f32[2,64,64]{0,2,1:T(8,128)S(1)}, s32[]{:T(128)}, s32[2]{0:T(128)S(1)}, /*index=5*/s32[1]{0:T(128)}, s32[3]{0:T(128)S(1)}, s32[]{:T(128)}, s32[]{:T(128)}) while((s32[]{:T(128)}, f32[2,64,64]{2,0,1:T(2,128)S(1)}, f32[2,64,64]{0,2,1:T(8,128)S(1)}, s32[]{:T(128)}, ...), condition=%wide.region_4.5_spmd.clone, body=%wide.region_1.4_spmd.clone.sunk | while | flops 197400 | bytes 75255 | solution.py:42
  351.3 57.6 %psum.23 = f32[2,32,32]{2,1,0:T(8,128)S(1)} all-reduce(f32[2,32,32]{2,1,0:T(8,128)S(1)} %fusion.80), channel_id=1, replica_groups=mesh['level'=2,'lon'=8,'lat'=2] {'lon','lat'}, use_global_device_ids=true, to_apply=%region_6.0 | all-reduce | flops 2048 | bytes 16384 | tf_op jit(solution)/shard_map/psum | solution.py:109
  409.3 131.4 %while.72 = (s32[]{:T(128)}, f32[2,32,32]{2,0,1:T(2,128)S(1)}, f32[2,32,32]{2,0,1:T(2,128)S(1)}, f32[2,32,32]{0,2,1:T(8,128)S(1)}, s32[]{:T(128)}, /*index=5*/s3...) while((s32[]{:T(128)}, f32[2,32,32]{2,0,1:T(2,128)S(1)}, ...), condition=%wide.region_10.11_spmd.clone, body=%wide.region_7.10_spmd.clone.sunk | while | flops 49752 | bytes 26751 | solution.py:42
  412.6 0.8 constant_dynamic-update-slice_fusion.5
  416.7 0.8 constant_dynamic-update-slice_fusion.5
  420.8 0.8 constant_dynamic-update-slice_fusion.5
  424.9 0.8 constant_dynamic-update-slice_fusion.5
  437.2 0.8 constant_dynamic-update-slice_fusion.5
  441.4 0.8 constant_dynamic-update-slice_fusion.5
  445.5 0.8 constant_dynamic-update-slice_fusion.5
  449.6 0.8 constant_dynamic-update-slice_fusion.5
  453.7 0.8 constant_dynamic-update-slice_fusion.5
  457.8 0.8 constant_dynamic-update-slice_fusion.5
  461.9 0.8 constant_dynamic-update-slice_fusion.5
  474.2 0.8 constant_dynamic-update-slice_fusion.5
  478.3 0.8 constant_dynamic-update-slice_fusion.5
  482.4 0.8 constant_dynamic-update-slice_fusion.5
  486.5 0.8 constant_dynamic-update-slice_fusion.5
  490.6 0.8 constant_dynamic-update-slice_fusion.5
  494.7 0.8 constant_dynamic-update-slice_fusion.5
  542.4 267.9 %while.73 = (s32[]{:T(128)}, f32[2,64,64]{2,0,1:T(2,128)S(1)}, f32[2,64,64]{0,2,1:T(8,128)S(1)}, s32[]{:T(128)}, s32[2]{0:T(128)S(1)}, /*index=5*/s32[1]{0:T(128)}, s32[3]{0:T(128)S(1)}, s32[]{:T(128)}, s32[]{:T(128)}) while((s32[]{:T(128)}, f32[2,64,64]{2,0,1:T(2,128)S(1)}, f32[2,64,64]{0,2,1:T(8,128)S(1)}, s32[]{:T(128)}, ...), condition=%wide.region_14.15_spmd.clone, body=%wide.region_11.14_spmd.clone.sunk | while | flops 197400 | bytes 75255 | solution.py:42
  811.8 267.9 %while.74 = (s32[]{:T(128)}, f32[2,64,64]{2,0,1:T(2,128)S(1)}, f32[2,64,64]{0,2,1:T(8,128)S(1)}, s32[]{:T(128)}, s32[2]{0:T(128)S(1)}, /*index=5*/s32[1]{0:T(128)}, s32[3]{0:T(128)S(1)}, s32[]{:T(128)}, s32[]{:T(128)}) while((s32[]{:T(128)}, f32[2,64,64]{2,0,1:T(2,128)S(1)}, f32[2,64,64]{0,2,1:T(8,128)S(1)}, s32[]{:T(128)}, ...), condition=%wide.region_18.19_spmd.clone, body=%wide.region_15.0_spmd.clone.sunk | while | flops 197400 | bytes 75255 | solution.py:42
  1082.3 0.8 reshape.449
  (2726 shorter events, 778.7 us)
Async XLA Ops:
  1.7 8.3 collective-permute-start
  7.7 6.6 collective-permute-start.1
  15.7 4.4 collective-permute-start.2
  17.0 4.0 collective-permute-start.3
  20.1 61.2 %copy-start = (s32[2]{0:T(128)S(1)}, s32[2]{0:T(128)}, u32[]{:S(2)}) copy-start(s32[2]{0:T(128)} %constant.357.clone.2) | copy-start | bytes 28
  20.1 61.2 %copy-start.1 = (s32[3]{0:T(128)S(1)}, s32[3]{0:T(128)}, u32[]{:S(2)}) copy-start(s32[3]{0:T(128)} %constant.358.clone.2) | copy-start | bytes 40
  81.2 328.1 %copy-start.2 = (s32[2]{0:T(128)S(1)}, s32[2]{0:T(128)}, u32[]{:S(2)}) copy-start(s32[2]{0:T(128)} %constant.365.clone.2) | copy-start | bytes 28
  81.2 328.1 %copy-start.3 = (s32[3]{0:T(128)S(1)}, s32[3]{0:T(128)}, u32[]{:S(2)}) copy-start(s32[3]{0:T(128)} %constant.366.clone.2) | copy-start | bytes 40
where the time goes:
time: 1090 us; the launch traced here: 1080 us
  other arithmetic  404 us (37%)
  local copies, waits for them, and re-layouts  308 us (28%)
  loops' own time  154 us (14%)
  blocking collectives  116 us (11%)
  matrix products  84 us (8%)
    while x448, local copies, waits for them, and re-layouts, row_step(): column = lax.dynamic_slice_in_dim(matrix, row, 1, 1)[:, 0]  286 us
    scatter x224, other arithmetic, row_step(): lax.dynamic_update_slice_in_dim(inverse, inverse_row[None], row, 0)  170 us
    another operation x224, other arithmetic  163 us
    another operation x4, loops' own time, cholesky_pair(): lax.fori_loop(0, order, row_step, (jnp.zeros_like(matrix), jnp.zeros_like...  154 us
    psum x1, blocking collectives, per_device(): sum_uu, sum_ua = lax.psum((local_uu, local_ua), ('lon', 'lat'))  58.7 us
    psum x1, blocking collectives, per_device(): sum_rr = lax.psum(local_rr, ('lon', 'lat'))  57.6 us
    dot_general x224, matrix products, row_step(): partial_row = jnp.dot(inverse, column, precision=FULL_PRECISION)  43.8 us
    dot_general x224, matrix products, row_step(): jnp.dot(partial_row, inverse, precision=FULL_PRECISION)  35.1 us
  transfers between devices with their start and end apart: 4, of which 2 were waited for; matrix products, arithmetic and copies ran while one was open for 0% of the time, Pallas kernels for 0%

commit v1 on v0

v1 whole, which is shorter than its diff:
```python
import functools
import numpy as np
import jax
import jax.numpy as jnp
from jax import lax
from jax.experimental import pallas as pl
from jax.experimental.pallas import tpu as pltpu
from jax.sharding import PartitionSpec as P

ITERS = 2
LANES = 128
EXACT = lax.Precision.HIGHEST


def mm(a, b):
    return lax.dot_general(
        a, b, (((1,), (0,)), ((), ())), precision=EXACT, preferred_element_type=jnp.float32
    )


def mm_nt(a, b):
    return lax.dot_general(
        a, b, (((1,), (1,)), ((), ())), precision=EXACT, preferred_element_type=jnp.float32
    )


def mm_tn(a, b):
    return lax.dot_general(
        a, b, (((0,), (0,)), ((), ())), precision=EXACT, preferred_element_type=jnp.float32
    )


def lane_ids(rows):
    return lax.broadcasted_iota(jnp.int32, (rows, LANES), 1)


def row_ids(rows):
    return lax.broadcasted_iota(jnp.int32, (rows, LANES), 0)


def rows_to(value, rows):
    return jnp.concatenate([value, jnp.zeros((rows - value.shape[0], LANES), jnp.float32)], axis=0)


def eliminate(systems, first_lane):
    order = systems[0][0].shape[0]
    sub = row_ids(8)
    blocks = [
        [[chunk[8 * t : 8 * t + 8] for t in range(order // 8)] for chunk in system]
        for system in systems
    ]
    results = [[[] for _ in system] for system in systems]
    for p in range(order // 8):
        for chunks, done in zip(blocks, results):
            lane = first_lane + 8 * p
            cols = [
                [
                    jnp.broadcast_to(chunks[0][t][:, lane + j : lane + j + 1], (8, LANES))
                    for t in range(p, order // 8)
                ]
                for j in range(8)
            ]
            head = [cols[j][0] for j in range(8)]
            rows = [chunk[p] for chunk in chunks]
            factor = [jnp.zeros((8, LANES), jnp.float32) for _ in chunks]
            for j in range(8):
                col = head[j]
                pivot = jnp.broadcast_to(col[j : j + 1], (8, LANES))
                inverse = 1.0 / pivot
                here = sub == j
                root = lax.rsqrt(pivot)
                root = root * (1.5 - 0.5 * pivot * root * root)
                for jj in range(j + 1, 8):
                    scaled = jnp.broadcast_to(head[jj][j : j + 1], (8, LANES)) * inverse
                    head[jj] = jnp.where(here, scaled, head[jj] - col * scaled)
                for i in range(len(rows)):
                    top = jnp.broadcast_to(rows[i][j : j + 1], (8, LANES))
                    factor[i] = jnp.where(here, top * root, factor[i])
                    scaled = top * inverse
                    rows[i] = jnp.where(here, scaled, rows[i] - col * scaled)
            for i in range(len(chunks)):
                done[i].append(factor[i])
            for i, chunk in enumerate(chunks):
                for j in range(8):
                    top = jnp.broadcast_to(rows[i][j : j + 1], (8, LANES))
                    for t in range(p + 1, order // 8):
                        chunk[t] = chunk[t] - cols[j][t - p] * top
    return [[jnp.concatenate(done, axis=0) for done in result] for result in results]


def small_problem(packed, values, rank, snaps):
    both = rank + snaps
    lanes = lane_ids(rank)
    rows = row_ids(rank)
    snap_lanes = (lanes >= rank) & (lanes < both)
    unit = jnp.where(lanes == rows, 1.0, 0.0).astype(jnp.float32)
    first = eliminate([[w, unit] for w in packed], 0)
    fields = range(len(packed))
    projected = [jnp.where(snap_lanes, first[f][0], 0.0) for f in fields]
    low_inverse = [first[f][1] for f in fields]
    s_lanes = lane_ids(snaps)
    s_rows = row_ids(snaps)
    s_unit = jnp.where(s_lanes == s_rows + rank, 1.0, 0.0).astype(jnp.float32)
    s_mask = (s_lanes >= rank) & (s_lanes < both)
    systems = []
    for f in fields:
        aa = pltpu.roll(packed[f][:snaps], LANES - snaps, 1)
        shared = mm_tn(projected[f], projected[f])[rank:both]
        systems.append([jnp.where(s_mask, aa - shared, 0.0), s_unit])
    second = eliminate(systems, rank)
    top, joint, square, low_all = [], [], [], []
    for f in fields:
        factor_up = jnp.where(s_lanes >= s_rows + rank, second[f][0], 0.0)
        up_inverse = second[f][1]
        top.append(jnp.where(lanes == rows, values[f], projected[f]))
        joint.append(rows_to(jnp.concatenate([top[f], factor_up], axis=0), LANES))
        lifted = mm_tn(projected[f], low_inverse[f])
        mixed = up_inverse - mm(up_inverse, lifted)
        low_all.append(rows_to(jnp.concatenate([low_inverse[f], mixed], axis=0), LANES))
    applied = [mm_nt(top[f], joint[f]) for f in fields]
    square = [mm_nt(joint[f], joint[f]) for f in fields]
    for sweep in range(ITERS):
        systems = [[mm_nt(applied[f], rows_to(applied[f], LANES)), applied[f]] for f in fields]
        subspace = [result[1] for result in eliminate(systems, 0)]
        if sweep < ITERS - 1:
            applied = [mm(subspace[f], square[f]) for f in fields]
    coefficients = [mm(subspace[f], low_all[f]) for f in fields]
    stretched = [mm(subspace[f], joint[f]) for f in fields]
    ones = jnp.ones((8, LANES), jnp.float32)
    energy = [mm_nt(ones, stretched[f] * stretched[f]) for f in fields]
    return coefficients, [jnp.sqrt(e[:1]) for e in energy]


def update_kernel(lons, packed_ref, basis_ref, fields_ref, values_ref, out_ref, new_values_ref):
    rank = values_ref.shape[1]
    snaps = fields_ref.shape[1]
    packed = [packed_ref[f] for f in range(2)]
    values = [values_ref[f : f + 1, :] for f in range(2)]
    values = [jnp.concatenate([v, jnp.zeros((1, LANES - rank), jnp.float32)], axis=1) for v in values]
    coefficients, new_values = small_problem(packed, values, rank, snaps)
    pad = jnp.zeros((LANES - rank - snaps, lons * LANES), jnp.float32)
    for f in range(2):
        basis = jnp.concatenate(
            [basis_ref[f, pl.ds(i, rank, stride=lons), :] for i in range(lons)], axis=1
        )
        cells = jnp.concatenate([basis, fields_ref[f], pad], axis=0)
        result = mm(coefficients[f], cells)
        for i in range(lons):
            out_ref[f, pl.ds(i, rank, stride=lons), :] = result[:, i * LANES : (i + 1) * LANES]
        new_values_ref[f : f + 1, :] = new_values[f]


def gram_kernel(
    lons, rank, snaps, count, lat_count, cell_count, reduce_here,
    wind_ref, basis_ref, cos_ref,
    fields_ref, sum_ref,
    send_low, send_high, send_lat, got_low, got_high, got_lat,
    local, parts, own, halo_send, halo_got, part_send, part_got, own_send, own_got,
):
    lon, lat = lax.axis_index("lon"), lax.axis_index("lat")
    size = count * lat_count
    me = lon * lat_count + lat

    def place(index):
        return {"lon": lax.div(index, lat_count), "lat": lax.rem(index, lat_count)}

    up = {"lon": lax.rem(lon + 1, count), "lat": lat}
    down = {"lon": lax.rem(lon + count - 1, count), "lat": lat}
    mate = {"lon": lon, "lat": 1 - lat}
    if reduce_here:
        peers = [place(lax.rem(me + o, size)) for o in range(1, size)]
    else:
        peers = [up, down, mate]
    barrier = pltpu.get_barrier_semaphore()
    for peer in peers:
        pl.semaphore_signal(barrier, inc=1, device_id=peer, device_id_type=pl.DeviceIdType.MESH)

    def wind(c, i):
        return wind_ref[c, pl.ds(i, snaps, stride=lons), :]

    lane = lane_ids(snaps)
    first_lat = lat == 0
    cosines = jnp.where(first_lat, cos_ref[0:1], cos_ref[1:2])
    half_over = jnp.where(first_lat, cos_ref[2:3], cos_ref[3:4])
    edge = jnp.zeros((snaps, LANES), jnp.float32)
    winds = [[wind(c, i) for i in range(lons)] for c in range(2)]
    weighted = [[w * cosines for w in line] for line in winds]
    for c in range(2):
        send_low[c] = winds[c][0]
        send_high[c] = winds[c][lons - 1]
        for i in range(lons):
            w = weighted[c][i]
            last = jnp.broadcast_to(w[:, LANES - 1 :], (snaps, LANES))
            first = jnp.broadcast_to(w[:, :1], (snaps, LANES))
            edge = jnp.where(lane == c * lons + i, jnp.where(first_lat, last, first), edge)
    send_lat[...] = edge
    pl.semaphore_wait(barrier, len(peers))

    def send(src, dst, sem, got, peer):
        copy = pltpu.make_async_remote_copy(
            src_ref=src, dst_ref=dst, send_sem=sem, recv_sem=got,
            device_id=peer, device_id_type=pl.DeviceIdType.MESH,
        )
        copy.start()
        return copy

    halo = [
        send(send_low, got_high, halo_send.at[0], halo_got.at[0], down),
        send(send_high, got_low, halo_send.at[1], halo_got.at[1], up),
        send(send_lat, got_lat, halo_send.at[2], halo_got.at[2], mate),
    ]
    bases = [
        jnp.concatenate([basis_ref[f, pl.ds(i, rank, stride=lons), :] for i in range(lons)], axis=1)
        for f in range(2)
    ]
    grams = [mm_nt(b, jnp.concatenate([b, jnp.zeros_like(b)], axis=0)) for b in bases]
    for copy in halo:
        copy.wait()
    side = got_lat[...]
    before = [got_low[c] for c in range(2)]
    after = [got_high[c] for c in range(2)]

    def lon_diff(c, i):
        nxt = winds[c][i + 1] if i < lons - 1 else after[c]
        prv = winds[c][i - 1] if i > 0 else before[c]
        return nxt - prv

    def lat_diff(c, i):
        w = weighted[c][i]
        k = c * lons + i
        outer = jnp.broadcast_to(side[:, k : k + 1], (snaps, LANES))
        nxt = pltpu.roll(w, LANES - 1, 1)
        prv = pltpu.roll(w, 1, 1)
        nxt = jnp.where(lane == LANES - 1, jnp.where(first_lat, outer, 0.0), nxt)
        prv = jnp.where(lane == 0, jnp.where(first_lat, 0.0, outer), prv)
        return nxt - prv

    for f in range(2):
        parts_of = []
        for i in range(lons):
            if f == 0:
                value = lon_diff(1, i) - lat_diff(0, i)
            else:
                value = lon_diff(0, i) + lat_diff(1, i)
            parts_of.append(value * half_over)
        field = jnp.concatenate(parts_of, axis=1)
        fields_ref[f] = field
        gap = jnp.zeros((rank, lons * LANES), jnp.float32)
        tail = jnp.zeros((LANES - rank - snaps, lons * LANES), jnp.float32)
        cross = mm_nt(bases[f], jnp.concatenate([gap, field, tail], axis=0))
        inner = mm_nt(field, jnp.concatenate([gap, tail, field], axis=0))
        packed = (grams[f] + cross + rows_to(inner, rank)) * (1.0 / cell_count)
        for t in range(rank // 8):
            if reduce_here:
                local[f * (rank // 8) + t] = packed[8 * t : 8 * t + 8]
            else:
                sum_ref[f * (rank // 8) + t] = packed[8 * t : 8 * t + 8]
    if not reduce_here:
        return
    copies = []
    for o in range(1, size):
        there = lax.rem(me + o, size)
        copies.append(
            send(local.at[there], parts.at[o - 1], part_send.at[o - 1], part_got.at[o - 1], peers[o - 1])
        )
    total = local[me]
    for o in range(1, size):
        copies[o - 1].wait_recv()
        total = total + parts[o - 1]
    own[...] = total
    sum_ref[me] = total
    gathers = []
    for o in range(1, size):
        gathers.append(
            send(own, sum_ref.at[me], own_send.at[o - 1], own_got.at[o - 1], peers[o - 1])
        )
    for o in range(1, size):
        copies[o - 1].wait_send()
    for o in range(1, size):
        source = lax.rem(me + size - o, size)
        pltpu.make_async_remote_copy(
            src_ref=own, dst_ref=sum_ref.at[source], send_sem=own_send.at[o - 1],
            recv_sem=own_got.at[o - 1], device_id=peers[o - 1], device_id_type=pl.DeviceIdType.MESH,
        ).wait_recv()
    for copy in gathers:
        copy.wait_send()


def per_device(wind_snaps, old_basis, old_values):
    snaps, rank = wind_snaps.shape[1], old_basis.shape[1]
    lons, lats = wind_snaps.shape[2:]
    count, lat_count = lax.axis_size("lon"), lax.axis_size("lat")
    size = count * lat_count
    rows_all = lats * lat_count
    cell_count = lons * count * rows_all
    assert lats == LANES and lat_count == 2 and count > 2 and rank + 2 * snaps == LANES
    place = np.arange(rows_all, dtype=np.float64)
    cosines = np.cos(((place + 0.5) / rows_all - 0.5) * (np.pi / 2.0))
    table = np.concatenate([cosines, 0.5 / cosines]).reshape(4, LANES)
    table = np.concatenate([table, np.zeros((4, LANES))]).astype(np.float32)
    tiles = 2 * rank // 8
    reduce_here = size == tiles
    wind_rows = wind_snaps.reshape(2, snaps * lons, LANES)
    basis_rows = old_basis.reshape(2, rank * lons, LANES)
    vmem = pl.BlockSpec(memory_space=pltpu.VMEM)
    many = size - 1 if reduce_here else 1
    fields, packed = pl.pallas_call(
        functools.partial(
            gram_kernel, lons, rank, snaps, count, lat_count, cell_count, reduce_here
        ),
        out_shape=(
            jax.ShapeDtypeStruct((2, snaps, lons * LANES), jnp.float32),
            jax.ShapeDtypeStruct((tiles, 8, LANES), jnp.float32),
        ),
        in_specs=[vmem] * 3,
        out_specs=(vmem, vmem),
        scratch_shapes=[
            pltpu.VMEM((2, snaps, LANES), jnp.float32),
            pltpu.VMEM((2, snaps, LANES), jnp.float32),
            pltpu.VMEM((snaps, LANES), jnp.float32),
            pltpu.VMEM((2, snaps, LANES), jnp.float32),
            pltpu.VMEM((2, snaps, LANES), jnp.float32),
            pltpu.VMEM((snaps, LANES), jnp.float32),
            pltpu.VMEM((tiles, 8, LANES), jnp.float32),
            pltpu.VMEM((many, 8, LANES), jnp.float32),
            pltpu.VMEM((8, LANES), jnp.float32),
            pltpu.SemaphoreType.DMA((3,)),
            pltpu.SemaphoreType.DMA((3,)),
            pltpu.SemaphoreType.DMA((many,)),
            pltpu.SemaphoreType.DMA((many,)),
            pltpu.SemaphoreType.DMA((many,)),
            pltpu.SemaphoreType.DMA((many,)),
        ],
        compiler_params=pltpu.CompilerParams(
            collective_id=0, has_side_effects=True, vmem_limit_bytes=16 * 2**20
        ),
        name="gram",
    )(wind_rows, basis_rows, jnp.asarray(table))
    if not reduce_here:
        packed = lax.psum(packed, ("lon", "lat"))
    new_basis, new_values = pl.pallas_call(
        functools.partial(update_kernel, lons),
        out_shape=(
            jax.ShapeDtypeStruct((2, rank * lons, LANES), jnp.float32),
            jax.ShapeDtypeStruct((2, rank), jnp.float32),
        ),
        in_specs=[vmem] * 4,
        out_specs=(vmem, vmem),
        compiler_params=pltpu.CompilerParams(vmem_limit_bytes=24 * 2**20),
        name="update",
    )(packed.reshape(2, rank, LANES), basis_rows, fields, old_values)
    return new_basis.reshape(2, rank, lons, LANES), new_values


def solution(mesh):
    placed = (P("level", None, "lon", "lat"), P("level", None, "lon", "lat"), P("level", None))
    return jax.shard_map(
        per_device,
        mesh=mesh,
        in_specs=placed,
        out_specs=(P("level", None, "lon", "lat"), P("level", None)),
        check_vma=False,
    )
```

time: 1090 us -> 34.5 us (0.03)
  other arithmetic: 404 us -> 0 us
  local copies, waits for them, and re-layouts: 308 us -> 3.2 us
  loops' own time: 154 us -> 0 us
  blocking collectives: 116 us -> 0 us
  matrix products: 84 us -> 0 us
  Pallas kernels: 0 us -> 30.4 us
    while x450 -> x0, local copies, waits for them, and re-layouts: 286 us -> none  [the longest x448 286 us: row_step(): column = lax.dynamic_slice_in_dim(matrix, row, 1, 1)[:, 0]]
    scatter x224 -> x0, other arithmetic: 170 us -> none  [row_step(): lax.dynamic_update_slice_in_dim(inverse, inverse_row[None], row, 0)]
    another operation x224 -> x0, other arithmetic: 163 us -> none
    another operation x4 -> x0, loops' own time: 154 us -> none  [cholesky_pair(): lax.fori_loop(0, order, row_step, (jnp.zeros_like(matrix), jnp.zeros_like...]
    psum x2 -> x0, blocking collectives: 116 us -> none  [the longest x1 58.7 us: per_device(): sum_uu, sum_ua = lax.psum((local_uu, local_ua), ('lon', 'lat'))]
    dot_general x466 -> x0, matrix products: 84 us -> none  [the longest x224 43.8 us: row_step(): partial_row = jnp.dot(inverse, column, precision=FULL_PRECISION)]
    pallas_call x0 -> x2, Pallas kernels: none -> 30.4 us  [the longest x1 19.3 us: per_device(): pl.pallas_call(functools.partial(gram_kernel, lons, rank, snaps, count, l...]
    reduce_sum x224 -> x0, other arithmetic: 30 us -> none  [row_step(): pivot = jnp.sqrt(diag_entry - jnp.sum(partial_row * partial_row))]
  transfers between devices with their start and end apart: 4 -> 0, of which waited for: 2 -> 0; matrix products, arithmetic and copies ran while one was open for 0% -> 0% of each run, Pallas kernels for 0% -> 0%
where the time goes in v1:
time: 34.5 us; the launch traced here: 34.3 us
  Pallas kernels  30.4 us (88%)
  local copies, waits for them, and re-layouts  3.2 us (9%)
  between operations  0.66 us (2%)
    pallas_call x1, Pallas kernels, per_device(): pl.pallas_call(functools.partial(gram_kernel, lons, rank, snaps, count, l...  19.3 us
    pallas_call x1, Pallas kernels, per_device(): pl.pallas_call(functools.partial(update_kernel, lons), out_shape=(jax.Sha...  11.2 us
    unnamed x10, local copies, waits for them, and re-layouts  3.2 us

profile of v1, /device:TPU:0, one launch (start us, length us, event | category | flops | bytes accessed | tf_op | source)
XLA Modules:
  0.0 34.3 jit_solution(8905741299483300112)
XLA Ops:
  0.6 0.0 copy-start
  0.6 0.9 %copy-done = f32[2,64,4,128]{3,2,1,0:T(4,128)S(1)} copy-done((f32[2,64,4,128]{3,2,1,0:T(4,128)S(1)}, f32[2,64,4,128]{3,2,1,0:T(4,128)}, u32[]{:S(2)}) %copy-start) | copy-done | bytes 262168
  1.6 0.0 copy-start.2
  1.6 0.9 %copy-done.2 = f32[2,32,4,128]{3,2,1,0:T(4,128)S(1)} copy-done((f32[2,32,4,128]{3,2,1,0:T(4,128)S(1)}, f32[2,32,4,128]{3,2,1,0:T(4,128)}, u32[]{:S(2)}) %copy-start.2) | copy-done | bytes 131096
  2.5 0.0 copy-start.3
  2.5 0.7 %copy-done.3 = f32[8,128]{1,0:T(8,128)S(1)} copy-done((f32[8,128]{1,0:T(8,128)S(1)}, f32[8,128]{1,0:T(8,128)}, u32[]{:S(2)}) %copy-start.3) | copy-done | bytes 4120
  3.2 0.0 copy-start.1
  3.2 19.3 %gram.1 = (f32[2,32,512]{2,1,0:T(8,128)S(1)}, f32[16,8,128]{2,1,0:T(8,128)S(1)}) custom-call(f32[2,128,128]{2,1,0:T(8,128)S(1)} %bitcast.6, f32[2,256,128]{2,1,0:T(8,128)S(1)} %bitcast.4, f32[8,128]{1,0:T(8,128)S(1)} %copy-done.3), custom_call_target="tpu_custom_call" | custom-call | tf_op jit(solution)/shard_map/gram/pallas_call | solution.py:307
  22.4 0.0 copy-start.4
  22.5 0.0 copy-done.1
  22.5 0.7 %copy-done.4 = f32[2,64]{1,0:T(2,128)S(1)} copy-done((f32[2,64]{1,0:T(2,128)S(1)}, f32[2,64]{1,0:T(2,128)}, u32[]{:S(2)}) %copy-start.4) | copy-done | bytes 536
  23.1 11.2 %update.1 = (f32[2,256,128]{2,1,0:T(8,128)}, f32[2,64]{1,0:T(2,128)}) custom-call(f32[2,64,128]{2,1,0:T(8,128)S(1)} %bitcast.7, f32[2,256,128]{2,1,0:T(8,128)S(1)} %bitcast.5, f32[2,32,512]{2,1,0:T(8,128)S(1)} %get-tuple-element.7.fields_ref, f32[2,64]{1,0:T(2,128)S(1)} %copy-done.4), custom_call_target="tpu_custom_call" | custom-call | tf_op jit(solution)/shard_map/update/pallas_call | solution.py:341
Async XLA Ops:
  0.6 1.0 %copy-start = (f32[2,64,4,128]{3,2,1,0:T(4,128)S(1)}, f32[2,64,4,128]{3,2,1,0:T(4,128)}, u32[]{:S(2)}) copy-start(f32[2,64,4,128]{3,2,1,0:T(4,128)} %param.5) | copy-start | bytes 786436
  1.6 0.9 %copy-start.2 = (f32[2,32,4,128]{3,2,1,0:T(4,128)S(1)}, f32[2,32,4,128]{3,2,1,0:T(4,128)}, u32[]{:S(2)}) copy-start(f32[2,32,4,128]{3,2,1,0:T(4,128)} %param.4) | copy-start | bytes 393220
  2.5 0.7 %copy-start.3 = (f32[8,128]{1,0:T(8,128)S(1)}, f32[8,128]{1,0:T(8,128)}, u32[]{:S(2)}) copy-start(f32[8,128]{1,0:T(8,128)} %constant.2.clone.cos_ref) | copy-start | bytes 12292
  3.2 19.3 %copy-start.1 = (f32[2,64,4,128]{3,2,1,0:T(4,128)S(1)}, f32[2,64,4,128]{3,2,1,0:T(4,128)}, u32[]{:S(2)}) copy-start(f32[2,64,4,128]{3,2,1,0:T(4,128)} %param.5) | copy-start | bytes 786436
  22.4 0.7 %copy-start.4 = (f32[2,64]{1,0:T(2,128)S(1)}, f32[2,64]{1,0:T(2,128)}, u32[]{:S(2)}) copy-start(f32[2,64]{1,0:T(2,128)} %values_ref.1) | copy-start | bytes 1540

commit v2 on v1

--- a/solution.py
+++ b/solution.py
@@ -131,31 +131,39 @@
     return coefficients, [jnp.sqrt(e[:1]) for e in energy]
 
 
-def update_kernel(lons, packed_ref, basis_ref, fields_ref, values_ref, out_ref, new_values_ref):
+def update(lons, packed, basis_ref, fields_ref, values_ref, finish, new_values_ref):
     rank = values_ref.shape[1]
     snaps = fields_ref.shape[1]
-    packed = [packed_ref[f] for f in range(2)]
     values = [values_ref[f : f + 1, :] for f in range(2)]
     values = [jnp.concatenate([v, jnp.zeros((1, LANES - rank), jnp.float32)], axis=1) for v in values]
     coefficients, new_values = small_problem(packed, values, rank, snaps)
     pad = jnp.zeros((LANES - rank - snaps, lons * LANES), jnp.float32)
     for f in range(2):
+        new_values_ref[f : f + 1, :] = new_values[f]
         basis = jnp.concatenate(
             [basis_ref[f, pl.ds(i, rank, stride=lons), :] for i in range(lons)], axis=1
         )
         cells = jnp.concatenate([basis, fields_ref[f], pad], axis=0)
-        result = mm(coefficients[f], cells)
+        finish(f, mm(coefficients[f], cells))
+
+
+def update_kernel(lons, packed_ref, basis_ref, fields_ref, values_ref, out_ref, new_values_ref):
+    rank = values_ref.shape[1]
+
+    def finish(f, result):
         for i in range(lons):
             out_ref[f, pl.ds(i, rank, stride=lons), :] = result[:, i * LANES : (i + 1) * LANES]
-        new_values_ref[f : f + 1, :] = new_values[f]
-
-
-def gram_kernel(
+
+    packed = [packed_ref[f] for f in range(2)]
+    update(lons, packed, basis_ref, fields_ref, values_ref, finish, new_values_ref)
+
+
+def gram_part(
     lons, rank, snaps, count, lat_count, cell_count, reduce_here,
-    wind_ref, basis_ref, cos_ref,
-    fields_ref, sum_ref,
-    send_low, send_high, send_lat, got_low, got_high, got_lat,
-    local, parts, own, halo_send, halo_got, part_send, part_got, own_send, own_got,
+    wind_hbm, basis_hbm, cos_hbm, values_hbm,
+    fields_ref, sum_ref, values_ref,
+    wind_ref, basis_ref, cos_ref, load_sem, send_low, send_high, send_lat, got_low, got_high, got_lat,
+    local, parts, by_layer, halo_send, halo_got, sends, gots,
 ):
     lon, lat = lax.axis_index("lon"), lax.axis_index("lat")
     size = count * lat_count
@@ -174,6 +182,17 @@
     barrier = pltpu.get_barrier_semaphore()
     for peer in peers:
         pl.semaphore_signal(barrier, inc=1, device_id=peer, device_id_type=pl.DeviceIdType.MESH)
+
+    loads = [
+        pltpu.make_async_copy(src, dst, load_sem.at[k])
+        for k, (src, dst) in enumerate(
+            [(wind_hbm, wind_ref), (cos_hbm, cos_ref), (basis_hbm, basis_ref), (values_hbm, values_ref)]
+        )
+    ]
+    for load in loads:
+        load.start()
+    loads[0].wait()
+    loads[1].wait()
 
     def wind(c, i):
         return wind_ref[c, pl.ds(i, snaps, stride=lons), :]
@@ -209,6 +228,7 @@
         send(send_high, got_low, halo_send.at[1], halo_got.at[1], up),
         send(send_lat, got_lat, halo_send.at[2], halo_got.at[2], mate),
     ]
+    loads[2].wait()
     bases = [
         jnp.concatenate([basis_ref[f, pl.ds(i, rank, stride=lons), :] for i in range(lons)], axis=1)
         for f in range(2)
@@ -247,43 +267,97 @@
         fields_ref[f] = field
         gap = jnp.zeros((rank, lons * LANES), jnp.float32)
         tail = jnp.zeros((LANES - rank - snaps, lons * LANES), jnp.float32)
-        cross = mm_nt(bases[f], jnp.concatenate([gap, field, tail], axis=0))
-        inner = mm_nt(field, jnp.concatenate([gap, tail, field], axis=0))
-        packed = (grams[f] + cross + rows_to(inner, rank)) * (1.0 / cell_count)
-        for t in range(rank // 8):
-            if reduce_here:
-                local[f * (rank // 8) + t] = packed[8 * t : 8 * t + 8]
-            else:
-                sum_ref[f * (rank // 8) + t] = packed[8 * t : 8 * t + 8]
+        right = mm_nt(jnp.concatenate([bases[f], field], axis=0), jnp.concatenate([gap, field, tail], axis=0))
+        inner = pltpu.roll(right[rank:], snaps, 1)
+        packed = (grams[f] + right[:rank] + rows_to(inner, rank)) * (1.0 / cell_count)
+        half = rank // 2
+        for t in range(2):
+            target = local if reduce_here else sum_ref
+            target[2 * f + t] = packed[half * t : half * t + half]
+    loads[3].wait()
     if not reduce_here:
         return
+    plane = lax.rem(lon, 2) * lat_count + lat
+    layer = lax.div(lon, 2)
+    layers = count // 2
+
+    def member(index):
+        return {"lon": layer * 2 + lax.div(index, 2), "lat": lax.rem(index, 2)}
+
+    def across(index):
+        return {"lon": index * 2 + lax.rem(lon, 2), "lat": lat}
+
     copies = []
-    for o in range(1, size):
-        there = lax.rem(me + o, size)
+    for o in range(1, 4):
+        there = lax.rem(plane + o, 4)
         copies.append(
-            send(local.at[there], parts.at[o - 1], part_send.at[o - 1], part_got.at[o - 1], peers[o - 1])
-        )
-    total = local[me]
-    for o in range(1, size):
+            send(local.at[there], parts.at[o - 1], sends.at[o - 1], gots.at[o - 1], member(there))
+        )
+    total = local[plane]
+    for o in range(1, 4):
         copies[o - 1].wait_recv()
         total = total + parts[o - 1]
-    own[...] = total
-    sum_ref[me] = total
+    by_layer[layer] = total
+    crossing = []
+    for o in range(1, layers):
+        there = lax.rem(layer + o, layers)
+        k = 2 + o
+        crossing.append(
+            send(by_layer.at[layer], by_layer.at[layer], sends.at[k], gots.at[k], across(there))
+        )
+    for o in range(1, layers):
+        there = lax.rem(layer + layers - o, layers)
+        k = 2 + o
+        pltpu.make_async_remote_copy(
+            src_ref=by_layer.at[layer], dst_ref=by_layer.at[there], send_sem=sends.at[k],
+            recv_sem=gots.at[k], device_id=across(there), device_id_type=pl.DeviceIdType.MESH,
+        ).wait_recv()
+    total = by_layer[0]
+    for z in range(1, layers):
+        total = total + by_layer[z]
+    sum_ref[plane] = total
     gathers = []
-    for o in range(1, size):
+    for o in range(1, 4):
+        there = lax.rem(plane + o, 4)
+        k = 1 + layers + o
         gathers.append(
-            send(own, sum_ref.at[me], own_send.at[o - 1], own_got.at[o - 1], peers[o - 1])
-        )
-    for o in range(1, size):
-        copies[o - 1].wait_send()
-    for o in range(1, size):
-        source = lax.rem(me + size - o, size)
+            send(sum_ref.at[plane], sum_ref.at[plane], sends.at[k], gots.at[k], member(there))
+        )
+    for o in range(1, 4):
+        there = lax.rem(plane + 4 - o, 4)
+        k = 1 + layers + o
         pltpu.make_async_remote_copy(
-            src_ref=own, dst_ref=sum_ref.at[source], send_sem=own_send.at[o - 1],
-            recv_sem=own_got.at[o - 1], device_id=peers[o - 1], device_id_type=pl.DeviceIdType.MESH,
+            src_ref=sum_ref.at[plane], dst_ref=sum_ref.at[there], send_sem=sends.at[k],
+            recv_sem=gots.at[k], device_id=member(there), device_id_type=pl.DeviceIdType.MESH,
         ).wait_recv()
-    for copy in gathers:
+    for copy in copies + crossing + gathers:
         copy.wait_send()
+
+
+def gram_kernel(*args):
+    gram_part(*args)
+
+
+def whole_kernel(*args):
+    config, rest = args[:7], args[7:]
+    inputs, (out_hbm, new_values_ref), scratch = rest[:4], rest[4:6], rest[6:]
+    fields_ref, sum_ref, values_ref, staged, out_sem = scratch[:5]
+    gram_part(*config, *inputs, fields_ref, sum_ref, values_ref, *scratch[5:])
+    basis_ref = scratch[6]
+    lons, rank = config[:2]
+    outgoing = []
+
+    def finish(f, result):
+        for i in range(lons):
+            staged[f, pl.ds(i, rank, stride=lons), :] = result[:, i * LANES : (i + 1) * LANES]
+        copy = pltpu.make_async_copy(staged.at[f], out_hbm.at[f], out_sem.at[f])
+        copy.start()
+        outgoing.append(copy)
+
+    packed = [jnp.concatenate([sum_ref[2 * f], sum_ref[2 * f + 1]], axis=0) for f in range(2)]
+    update(lons, packed, basis_ref, fields_ref, values_ref, finish, new_values_ref)
+    for copy in outgoing:
+        copy.wait()
 
 
 def per_device(wind_snaps, old_basis, old_values):
@@ -298,57 +372,71 @@
     cosines = np.cos(((place + 0.5) / rows_all - 0.5) * (np.pi / 2.0))
     table = np.concatenate([cosines, 0.5 / cosines]).reshape(4, LANES)
     table = np.concatenate([table, np.zeros((4, LANES))]).astype(np.float32)
-    tiles = 2 * rank // 8
-    reduce_here = size == tiles
+    reduce_here = size <= 16 and count % 2 == 0
     wind_rows = wind_snaps.reshape(2, snaps * lons, LANES)
     basis_rows = old_basis.reshape(2, rank * lons, LANES)
     vmem = pl.BlockSpec(memory_space=pltpu.VMEM)
-    many = size - 1 if reduce_here else 1
-    fields, packed = pl.pallas_call(
-        functools.partial(
-            gram_kernel, lons, rank, snaps, count, lat_count, cell_count, reduce_here
-        ),
-        out_shape=(
-            jax.ShapeDtypeStruct((2, snaps, lons * LANES), jnp.float32),
-            jax.ShapeDtypeStruct((tiles, 8, LANES), jnp.float32),
-        ),
-        in_specs=[vmem] * 3,
-        out_specs=(vmem, vmem),
-        scratch_shapes=[
-            pltpu.VMEM((2, snaps, LANES), jnp.float32),
-            pltpu.VMEM((2, snaps, LANES), jnp.float32),
-            pltpu.VMEM((snaps, LANES), jnp.float32),
-            pltpu.VMEM((2, snaps, LANES), jnp.float32),
-            pltpu.VMEM((2, snaps, LANES), jnp.float32),
-            pltpu.VMEM((snaps, LANES), jnp.float32),
-            pltpu.VMEM((tiles, 8, LANES), jnp.float32),
-            pltpu.VMEM((many, 8, LANES), jnp.float32),
-            pltpu.VMEM((8, LANES), jnp.float32),
-            pltpu.SemaphoreType.DMA((3,)),
-            pltpu.SemaphoreType.DMA((3,)),
-            pltpu.SemaphoreType.DMA((many,)),
-            pltpu.SemaphoreType.DMA((many,)),
-            pltpu.SemaphoreType.DMA((many,)),
-            pltpu.SemaphoreType.DMA((many,)),
-        ],
-        compiler_params=pltpu.CompilerParams(
-            collective_id=0, has_side_effects=True, vmem_limit_bytes=16 * 2**20
-        ),
+    hbm = pl.BlockSpec(memory_space=pltpu.HBM)
+    scratch = [
+        pltpu.VMEM((2, snaps * lons, LANES), jnp.float32),
+        pltpu.VMEM((2, rank * lons, LANES), jnp.float32),
+        pltpu.VMEM((8, LANES), jnp.float32),
+        pltpu.SemaphoreType.DMA((4,)),
+        pltpu.VMEM((2, snaps, LANES), jnp.float32),
+        pltpu.VMEM((2, snaps, LANES), jnp.float32),
+        pltpu.VMEM((snaps, LANES), jnp.float32),
+        pltpu.VMEM((2, snaps, LANES), jnp.float32),
+        pltpu.VMEM((2, snaps, LANES), jnp.float32),
+        pltpu.VMEM((snaps, LANES), jnp.float32),
+        pltpu.VMEM((4, rank // 2, LANES), jnp.float32),
+        pltpu.VMEM((3, rank // 2, LANES), jnp.float32),
+        pltpu.VMEM((count // 2, rank // 2, LANES), jnp.float32),
+        pltpu.SemaphoreType.DMA((3,)),
+        pltpu.SemaphoreType.DMA((3,)),
+        pltpu.SemaphoreType.DMA((5 + count // 2,)),
+        pltpu.SemaphoreType.DMA((5 + count // 2,)),
+    ]
+    gram_out = [(2, snaps, lons * LANES), (4, rank // 2, LANES), (2, rank)]
+    out_shape = (
+        jax.ShapeDtypeStruct((2, rank * lons, LANES), jnp.float32),
+        jax.ShapeDtypeStruct((2, rank), jnp.float32),
+    )
+    config = (lons, rank, snaps, count, lat_count, cell_count, reduce_here)
+    inputs = (wind_rows, basis_rows, jnp.asarray(table), old_values)
+    params = pltpu.CompilerParams(
+        collective_id=0, has_side_effects=True, vmem_limit_bytes=62 * 2**20
+    )
+    if reduce_here:
+        new_basis, new_values = pl.pallas_call(
+            functools.partial(whole_kernel, *config),
+            out_shape=out_shape,
+            in_specs=[hbm] * 4,
+            out_specs=(hbm, vmem),
+            scratch_shapes=[pltpu.VMEM(shape, jnp.float32) for shape in gram_out]
+            + [pltpu.VMEM(out_shape[0].shape, jnp.float32), pltpu.SemaphoreType.DMA((2,))]
+            + scratch,
+            compiler_params=params,
+            name="whole",
+        )(*inputs)
+        return new_basis.reshape(2, rank, lons, LANES), new_values
+    fields, packed, values = pl.pallas_call(
+        functools.partial(gram_kernel, *config),
+        out_shape=tuple(jax.ShapeDtypeStruct(shape, jnp.float32) for shape in gram_out),
+        in_specs=[hbm] * 4,
+        out_specs=(vmem, vmem, vmem),
+        scratch_shapes=scratch,
+        compiler_params=params,
         name="gram",
-    )(wind_rows, basis_rows, jnp.asarray(table))
-    if not reduce_here:
-        packed = lax.psum(packed, ("lon", "lat"))
+    )(*inputs)
+    packed = lax.psum(packed, ("lon", "lat"))
     new_basis, new_values = pl.pallas_call(
         functools.partial(update_kernel, lons),
-        out_shape=(
-            jax.ShapeDtypeStruct((2, rank * lons, LANES), jnp.float32),
-            jax.ShapeDtypeStruct((2, rank), jnp.float32),
-        ),
+        out_shape=out_shape,
         in_specs=[vmem] * 4,
         out_specs=(vmem, vmem),
         compiler_params=pltpu.CompilerParams(vmem_limit_bytes=24 * 2**20),
         name="update",
-    )(packed.reshape(2, rank, LANES), basis_rows, fields, old_values)
+    )(packed.reshape(2, rank, LANES), basis_rows, fields, values)
     return new_basis.reshape(2, rank, lons, LANES), new_values
 
 

time: 34.5 us -> 34.1 us (0.988)
  local copies, waits for them, and re-layouts: 3.2 us -> 2.24 us
  Pallas kernels: 30.4 us -> 31.1 us
    unnamed x10 -> x4, local copies, waits for them, and re-layouts: 3.2 us -> 2.24 us
    pallas_call x2 -> x1, Pallas kernels: 30.4 us -> 31.1 us  [per_device(): pl.pallas_call(functools.partial(whole_kernel, *config), out_shape=out_sh...]
where the time goes in v2:
time: 34.1 us; the launch traced here: 34 us
  Pallas kernels  31.1 us (91%)
  local copies, waits for them, and re-layouts  2.24 us (7%)
  between operations  0.65 us (2%)
    pallas_call x1, Pallas kernels, per_device(): pl.pallas_call(functools.partial(whole_kernel, *config), out_shape=out_sh...  31.1 us
    unnamed x4, local copies, waits for them, and re-layouts  2.24 us

profile of v2, /device:TPU:0, one launch (start us, length us, event | category | flops | bytes accessed | tf_op | source)
XLA Modules:
  0.0 34.0 jit_solution(9690628809474229284)
XLA Ops:
  0.6 31.1 %whole.1 = (f32[2,256,128]{2,1,0:T(8,128)}, f32[2,64]{1,0:T(2,128)}) custom-call(f32[2,128,128]{2,1,0:T(8,128)} %bitcast.5, f32[2,256,128]{2,1,0:T(8,128)} %bitcast.3, f32[8,128]{1,0:T(8,128)} %constant.2.clone.args_2_, f32[2,64]{1,0:T(2,128)} %args_3_.1), custom_call_target="tpu_custom_call" | custom-call | tf_op jit(solution)/shard_map/whole/pallas_call | solution.py:410
  31.7 0.0 copy-start
  31.7 1.7 %copy.8 = f32[2,64,4,128]{3,2,1,0:T(4,128)} copy(f32[2,64,4,128]{3,2,1,0:T(4,128)} %bitcast.4) | data formatting | bytes 524288
  33.4 0.0 copy-done
  33.4 0.6 %copy.9 = f32[2,64]{1,0:T(2,128)} copy(f32[2,64]{1,0:T(2,128)S(1)} %copy-done) | data formatting | bytes 1024
Async XLA Ops:
  31.7 1.7 %copy-start = (f32[2,64]{1,0:T(2,128)S(1)}, f32[2,64]{1,0:T(2,128)}, u32[]{:S(2)}) copy-start(f32[2,64]{1,0:T(2,128)} %get-tuple-element.9) | copy-start | bytes 1540
